TPU v7x, 256 devices: a whole 4x4x8 slice. The times are simulated.
256 devices in a mesh: node: 16 (over z, core), fsdp: 16 (over x, y).
Axes of the slice: x: 4, y: 4, z: 8, core: 2. Of those that a mesh axis runs over, the one named last changes fastest.
Arguments:
- hidden: bfloat16 [32768, 8192], P(('node', 'fsdp')), may hold values from -6 to 6
- queries: bfloat16 [32768, 4096], P(('node', 'fsdp')), may hold values from -70 to 70
- key_matrix: bfloat16 [8192, 512], P('fsdp'), may hold values from -0.0625 to 0.0625
- value_matrix: bfloat16 [8192, 512], P('fsdp'), may hold values from -0.0625 to 0.0625
- out_weight: bfloat16 [4096, 8192], P('fsdp'), may hold values from -0.25 to 0.25
- lengths: int32 [16, 8], P('node'), may hold values from 1 to 512, 2048 in all within a row
Outputs:
- updated: float32 [32768, 8192], P(('node', 'fsdp'))
All inputs are finite; a program needn't handle non-finite values.
Results may differ from a plain program's by a relative error of at most 0.0095.
Values may be sent and summed in bfloat16 or wider, within the bound.
A program may use at most 128 MiB of HBM per device.

v0:
```python
import jax
import jax.numpy as jnp
from jax import lax
from jax.sharding import PartitionSpec as P

HEAD_WIDTH = 128


def from_behind(value, axis, steps):
    count = lax.axis_size(axis)
    initial, last = (max(0, -steps), min(count, count - steps))
    return lax.ppermute(value, axis, [(source, source + steps) for source in range(initial, last)])


def body(hidden, queries, key_matrix, value_matrix, out_weight, lengths):
    tok_rows = hidden.shape[0]
    kv_width = key_matrix.shape[1]
    q_width = queries.shape[1]
    heads_kv = kv_width // HEAD_WIDTH
    query_group = q_width // HEAD_WIDTH // heads_kv
    reach = lax.axis_size("fsdp") // 4
    index = lax.axis_index("fsdp")
    hidden32 = hidden.astype(jnp.float32)
    scale_rows = lax.rsqrt(jnp.mean(hidden32 * hidden32, axis=1, keepdims=True) + 1e-05)
    normed = (hidden32 * scale_rows).astype(jnp.bfloat16)
    keys32 = jnp.dot(
        normed,
        lax.all_gather(key_matrix, "fsdp", axis=0, tiled=True),
        preferred_element_type=jnp.float32,
    )
    values32 = jnp.dot(
        normed,
        lax.all_gather(value_matrix, "fsdp", axis=0, tiled=True),
        preferred_element_type=jnp.float32,
    )
    local = jnp.stack([keys32.astype(jnp.bfloat16), values32.astype(jnp.bfloat16)])
    blocks = [local]
    for back in range(1, reach + 1):
        blocks.insert(0, from_behind(local, "fsdp", back))
    window = jnp.concatenate(blocks, axis=1)
    span = window.shape[1]
    ends = jnp.cumsum(lengths[0])
    query_pos = index * tok_rows + jnp.arange(tok_rows, dtype=jnp.int32)
    key_pos = (index - reach) * tok_rows + jnp.arange(span, dtype=jnp.int32)
    query_seg = jnp.sum((query_pos[:, None] >= ends[None, :]).astype(jnp.int32), axis=1)
    key_seg = jnp.sum((key_pos[:, None] >= ends[None, :]).astype(jnp.int32), axis=1)
    allowed = (
        (key_pos[None, :] >= 0)
        & (key_pos[None, :] <= query_pos[:, None])
        & (key_seg[None, :] == query_seg[:, None])
    )
    heads_of_query = queries.reshape(tok_rows, heads_kv, query_group, HEAD_WIDTH)
    heads_of_key = window[0].reshape(span, heads_kv, HEAD_WIDTH)
    heads_of_value = window[1].reshape(span, heads_kv, HEAD_WIDTH)
    scores = jnp.einsum(
        "tkgd,skd->kgts", heads_of_query, heads_of_key, preferred_element_type=jnp.float32
    ) / jnp.sqrt(jnp.float32(HEAD_WIDTH))
    scores = jnp.where(allowed[None, None], scores, jnp.float32(-1e30))
    top = jnp.max(scores, axis=3, keepdims=True)
    weights = jnp.where(allowed[None, None], jnp.exp(scores - top), jnp.float32(0.0))
    total = jnp.sum(weights, axis=3)
    rounded = weights.astype(jnp.bfloat16)
    mixed = jnp.einsum(
        "kgts,skd->tkgd", rounded, heads_of_value, preferred_element_type=jnp.float32
    )
    mixed = mixed / jnp.transpose(total, (2, 0, 1))[..., None]
    attention = mixed.reshape(tok_rows, q_width).astype(jnp.bfloat16)
    nodes = lax.axis_size("node")
    band_width = out_weight.shape[1] // nodes
    band = lax.dynamic_slice_in_dim(out_weight, lax.axis_index("node") * band_width, band_width, 1)
    band_rows = lax.all_gather(band, "fsdp", axis=0, tiled=True)
    partial_value = jnp.dot(
        lax.all_gather(attention, "node", axis=0, tiled=True),
        band_rows,
        preferred_element_type=jnp.float32,
    )
    projected = lax.all_to_all(
        partial_value.astype(jnp.bfloat16), "node", split_axis=0, concat_axis=1, tiled=True
    ).astype(partial_value.dtype)
    return hidden32 + projected


def solution(mesh):
    placed = (
        P(("node", "fsdp"), None),
        P(("node", "fsdp"), None),
        P("fsdp", None),
        P("fsdp", None),
        P("fsdp", None),
        P("node", None),
    )
    return jax.shard_map(
        body, mesh=mesh, in_specs=placed, out_specs=P(("node", "fsdp"), None), check_vma=False
    )
```

profile of v0, /device:TPU:1, one launch (start us, length us, event | category | flops | bytes accessed | tf_op | source)
XLA Modules:
  0.0 413.9 jit_solution(5463416138677280778)
XLA Ops:
  6.5 0.0 all-gather.7.cloned.1.call-start
  6.5 0.7 all-gather.7.cloned.1.call-update
  7.3 0.0 all-gather.5.cloned.1.call-start
  7.3 0.7 all-gather.5.cloned.1.call-update
  8.0 0.0 all-gather.11.cloned.1.call-start
  8.1 1.7 constant_dynamic-slice_fusion
  9.7 0.0 all-gather.11.cloned.1.call-update
  9.7 0.0 all-gather.9.cloned.1.call-start
  9.8 0.8 reduce-window.8
  10.6 0.1 convert_reduce_fusion.1
  10.7 0.1 convert_reduce_fusion
  10.8 2.1 fusion.7
  12.9 0.0 copy-start
  12.9 76.5 %all-gather.7.cloned.1.call-done = bf16[8192,512]{1,0:T(8,128)(2,1)} async-done(((bf16[512,512]{1,0:T(8,128)(2,1)}), bf16[8192,512]{1,0:T(8,128)(2,1)}) %all-gather.7.cloned.1.call-update) | async-done | bytes 8388624 | tf_op jit(solution)/shard_map/all_gather | solution.py:33
  89.4 5.3 %fusion.13 = bf16[1,128,512]{2,1,0:T(8,128)(2,1)S(1)} fusion(bf16[8192,512]{1,0:T(8,128)(2,1)} %all-gather.7.cloned.1.call-done, bf16[128,8192]{1,0:T(8,128)(2,1)} %param.6, f32[128]{0:T(128)S(1)} %add_rsqrt_fusion), kind=kOutput, calls=%fused_computation.21 | convolution fusion | flops 1076953088 | bytes 10617344 | tf_op jit(solution)/shard_map/dot_general | solution.py:31
  94.7 0.0 copy-start.1
  94.7 72.6 %all-gather.5.cloned.1.call-done = bf16[8192,512]{1,0:T(8,128)(2,1)} async-done(((bf16[512,512]{1,0:T(8,128)(2,1)}), bf16[8192,512]{1,0:T(8,128)(2,1)}) %all-gather.5.cloned.1.call-update) | async-done | bytes 8388624 | tf_op jit(solution)/shard_map/all_gather | solution.py:28
  167.3 0.0 copy-done
  167.3 4.7 %fusion.12 = bf16[1,128,512]{2,1,0:T(8,128)(2,1)S(1)} fusion(bf16[8192,512]{1,0:T(8,128)(2,1)} %all-gather.5.cloned.1.call-done, bf16[128,8192]{1,0:T(8,128)(2,1)S(1)} %copy-done, f32[128]{0:T(128)S(1)} %add_rsqrt_fusion), kind=kOutput, calls=%fused_computation.20 | convolution fusion | flops 1076953088 | bytes 10617344 | tf_op jit(solution)/shard_map/dot_general | solution.py:26
  172.1 3.1 collective-permute-start
  175.2 3.4 collective-permute-start.2
  178.6 3.7 collective-permute-start.1
  182.3 0.3 compare_and_fusion
  182.6 0.0 copy-done.1
  182.6 1.2 copy.24
  183.8 2.4 collective-permute-start.3
  186.2 0.0 collective-permute-done
  186.2 7.3 %collective-permute-done.1 = bf16[2,128,512]{2,1,0:T(8,128)(2,1)S(1)} collective-permute-done((bf16[2,128,512]{2,1,0:T(8,128)(2,1)S(1)}, bf16[2,128,512]{2,1,0:T(8,128)(2,1)S(1)}, u32[]{:S(2)}, u32[]{:S(2)}) %collective-permute-start.1) | collective-permute-done | bytes 262176 | tf_op jit(solution)/shard_map/ppermute | solution.py:12
  193.6 0.0 collective-permute-done.2
  193.6 0.0 collective-permute-done.3
  193.7 0.1 fusion.31
  193.8 1.0 reshape_squeeze.7
  194.8 0.3 copy.20
  195.1 8.5 %fusion.32 = (f32[4,8,128]{2,1,0:T(8,128)S(1)}, bf16[4,8,128,640]{2,3,1,0:T(8,128)(2,1)}) fusion(pred[128,640]{0,1:T(8,128)(4,1)S(1)} %compare_and_fusion, bf16[128,4,8,128]{3,2,1,0:T(8,128)(2,1)} %bitcast.46, bf16[640,4,128,1]{2,1,0,3:T(4,128)(2,1)} %bitcast.48), kind=kOutput, calls=%fused_computation.45 | convolution fusion | flops 686817920 | bytes 7045120 | tf_op jit(solution)/shard_map/sub | solution.py:60
  203.6 4.4 %fusion.9 = bf16[128,4,8,128]{0,3,2,1:T(8,128)(2,1)} fusion(bf16[640,4,128,1]{0,2,3,1:T(8,128)(2,1)S(1)} %bitcast.49, bf16[4,8,128,640]{2,3,1,0:T(8,128)(2,1)} %get-tuple-element.8, f32[128,4,8]{0,2,1:T(8,128)S(1)} %bitcast.53), kind=kOutput, calls=%fused_computation.17 | convolution fusion | flops 672137216 | bytes 6963200 | tf_op jit(solution)/shard_map/kgts,skd->tkgd/dot_general | solution.py:63
  208.0 0.0 all-gather.9.cloned.1.call-update
  208.1 21.5 %all-gather.11.cloned.1.call-done = bf16[4096,512]{1,0:T(8,128)(2,1)} async-done(((bf16[256,512]{1,0:T(8,128)(2,1)}), bf16[4096,512]{1,0:T(8,128)(2,1)}) %all-gather.11.cloned.1.call-update) | async-done | bytes 4194320 | tf_op jit(solution)/shard_map/all_gather | solution.py:71
  229.6 104.7 %all-gather.9.cloned.1.call-done = bf16[2048,4096]{0,1:T(8,128)(2,1)} async-done(((bf16[128,4096]{0,1:T(8,128)(2,1)}), bf16[2048,4096]{0,1:T(8,128)(2,1)}) %all-gather.9.cloned.1.call-update) | async-done | bytes 16777232 | tf_op jit(solution)/shard_map/all_gather | solution.py:73
  334.2 13.6 %convolution_convert_fusion = bf16[2048,512]{1,0:T(8,128)(2,1)S(1)} fusion(bf16[2048,4096]{0,1:T(8,128)(2,1)} %all-gather.9.cloned.1.call-done, bf16[4096,512]{1,0:T(8,128)(2,1)} %all-gather.11.cloned.1.call-done), kind=kOutput, calls=%fused_computation.15 | convolution fusion | flops 8590983168 | bytes 23068672 | tf_op jit(solution)/shard_map/dot_general | solution.py:72
  347.9 55.8 %all_to_all.13 = bf16[16,128,512]{2,1,0:T(8,128)(2,1)S(1)} all-to-all(bf16[16,128,512]{2,1,0:T(8,128)(2,1)S(1)} %bitcast.44), channel_id=1, replica_groups=mesh['node'=16,'fsdp'=16] {'node'}, dimensions={0} | all-to-all | bytes 4194304 | tf_op jit(solution)/shard_map/all_to_all | solution.py:77
  403.7 0.6 convert_bitcast_fusion
  404.3 0.5 copy.23
  404.8 2.6 convert_add_fusion
  (10 shorter events, 0.1 us)
Async XLA Ops:
  6.5 82.8 %all-gather.7.cloned.1.call-start = ((), (), s32[]{:S(2)}) async-start(), calls=%async_computation.2 | async-start | bytes 8912896 | tf_op jit(solution)/shard_map/all_gather | solution.py:33
  7.3 160.1 %all-gather.5.cloned.1.call-start = ((), (), s32[]{:S(2)}) async-start(), calls=%async_computation.1 | async-start | bytes 8912896 | tf_op jit(solution)/shard_map/all_gather | solution.py:28
  8.0 221.6 %all-gather.11.cloned.1.call-start = ((), (), s32[]{:S(2)}) async-start(), calls=%async_computation.4 | async-start | bytes 4456448 | tf_op jit(solution)/shard_map/all_gather | solution.py:71
  9.7 324.5 %all-gather.9.cloned.1.call-start = ((), (), s32[]{:S(2)}) async-start(), calls=%async_computation.3 | async-start | bytes 17825792 | tf_op jit(solution)/shard_map/all_gather | solution.py:73
  12.9 154.4 %copy-start = (bf16[128,8192]{1,0:T(8,128)(2,1)S(1)}, bf16[128,8192]{1,0:T(8,128)(2,1)}, u32[]{:S(2)}) copy-start(bf16[128,8192]{1,0:T(8,128)(2,1)} %param.6) | copy-start | bytes 6291460
  94.7 87.9 %copy-start.1 = (bf16[128,4096]{1,0:T(8,128)(2,1)S(1)}, bf16[128,4096]{1,0:T(8,128)(2,1)}, u32[]{:S(2)}) copy-start(bf16[128,4096]{1,0:T(8,128)(2,1)} %param.7) | copy-start | bytes 3145732
  172.1 14.1 %collective-permute-start = (bf16[2,128,512]{2,1,0:T(8,128)(2,1)S(1)}, bf16[2,128,512]{2,1,0:T(8,128)(2,1)S(1)}, u32[]{:S(2)}, u32[]{:S(2)}) collective-permute-start(bf16[2,128,512]{2,1,0:T(8,128)(2,1)S(1)} %pad_maximum_fusion), channel_id=1, source_target_pairs={{0,4},{1,5},{2,6},{3,7},{4,8},{5,9},{6,10},{7,11},{8,12},{9,13},{1... | collective-permute-start | bytes 786440 | tf_op jit(solution)/shard_map/ppermute | solution.py:12
  175.2 18.4 %collective-permute-start.2 = (bf16[2,128,512]{2,1,0:T(8,128)(2,1)S(1)}, bf16[2,128,512]{2,1,0:T(8,128)(2,1)S(1)}, u32[]{:S(2)}, u32[]{:S(2)}) collective-permute-start(bf16[2,128,512]{2,1,0:T(8,128)(2,1)S(1)} %pad_maximum_fusion), channel_id=1, source_target_pairs={{0,2},{1,3},{2,4},{3,5},{4,6},{5,7},{6,8},{7,9},{8,10},{9,11},{10,... | collective-permute-start | bytes 786440 | tf_op jit(solution)/shard_map/ppermute | solution.py:12
  178.6 15.0 %collective-permute-start.1 = (bf16[2,128,512]{2,1,0:T(8,128)(2,1)S(1)}, bf16[2,128,512]{2,1,0:T(8,128)(2,1)S(1)}, u32[]{:S(2)}, u32[]{:S(2)}) collective-permute-start(bf16[2,128,512]{2,1,0:T(8,128)(2,1)S(1)} %pad_maximum_fusion), channel_id=1, source_target_pairs={{0,3},{1,4},{2,5},{3,6},{4,7},{5,8},{6,9},{7,10},{8,11},{9,12},{10... | collective-permute-start | bytes 786440 | tf_op jit(solution)/shard_map/ppermute | solution.py:12
  183.8 9.8 %collective-permute-start.3 = (bf16[2,128,512]{2,1,0:T(8,128)(2,1)S(1)}, bf16[2,128,512]{2,1,0:T(8,128)(2,1)S(1)}, u32[]{:S(2)}, u32[]{:S(2)}) collective-permute-start(bf16[2,128,512]{2,1,0:T(8,128)(2,1)S(1)} %pad_maximum_fusion), channel_id=1, source_target_pairs={{0,1},{1,2},{2,3},{3,4},{4,5},{5,6},{6,7},{7,8},{8,9},{9,10},{10,1... | collective-permute-start | bytes 786440 | tf_op jit(solution)/shard_map/ppermute | solution.py:12
Sparse Core Ops, SparseCore 0:
  9.8 79.5 all-gather.6
  91.8 75.4 all-gather.4
  169.8 59.7 all-gather.10
  231.2 103.0 all-gather.8
where the time goes:
time: 414 us
  waiting for transfers between devices  284 us (69%)
  blocking collectives  55.8 us (13%)
  matrix products  36.6 us (9%)
  between operations  13.3 us (3%)
  starting transfers between devices  12.7 us (3%)
  other arithmetic  6.6 us (2%)
  local copies, waits for them, and re-layouts  4.83 us (1%)
    all_gather x1, waiting for transfers between devices, body(): lax.all_gather(attention, 'node', axis=0, tiled=True)  105 us
    all_gather x1, waiting for transfers between devices, body(): lax.all_gather(value_matrix, 'fsdp', axis=0, tiled=True)  76.5 us
    all_gather x1, waiting for transfers between devices, body(): lax.all_gather(key_matrix, 'fsdp', axis=0, tiled=True)  72.6 us
    all_to_all x1, blocking collectives, body(): lax.all_to_all(partial_value.astype(jnp.bfloat16), 'node', split_axis=0,...  55.8 us
    all_gather x1, waiting for transfers between devices, body(): band_rows = lax.all_gather(band, 'fsdp', axis=0, tiled=True)  21.5 us
    dot_general x1, matrix products, body(): jnp.dot(lax.all_gather(attention, 'node', axis=0, tiled=True), band_rows,...  13.6 us
    ppermute x4, starting transfers between devices, from_behind(): lax.ppermute(value, axis, [(source, source + steps) for source in range(i...  12.6 us
    sub x1, matrix products, body(): scores - top  8.5 us
  transfers between devices with their start and end apart: 8, of which 5 were waited for; matrix products, arithmetic and copies ran while one was open for 7% of the time, Pallas kernels for 0%

commit v1 on v0

v1 whole, which is shorter than its diff:
```python
import jax
import jax.numpy as jnp
from jax import lax
from jax.experimental import pallas as pl
from jax.experimental.pallas import tpu as pltpu
from jax.sharding import PartitionSpec as P

MESH = pl.DeviceIdType.MESH
HEAD = 128
TOK = 128
SLOTS = 8
COLS = 256
F32 = jnp.float32
BF16 = jnp.bfloat16


def gather_copies(buf, ssem, rsem, place, peers):
    x, y = place
    to_x, to_y = peers

    def copy(index, ref, device):
        return pltpu.make_async_remote_copy(
            src_ref=ref, dst_ref=ref, send_sem=ssem.at[index], recv_sem=rsem.at[index],
            device_id=device, device_id_type=MESH,
        )

    xr, xl = lax.rem(x + 1, 4), lax.rem(x + 3, 4)
    yr, yl = lax.rem(y + 1, 4), lax.rem(y + 3, 4)
    first = [copy(k, buf.at[x, 0, y], to_x[k]) for k in range(3)]
    first += [copy(3 + k, buf.at[x, 1, y], to_y[k]) for k in range(3)]
    second = [copy(6 + k, buf.at[:, 0, y], to_y[k]) for k in range(2)]
    second += [copy(8 + k, buf.at[x, 1], to_x[k]) for k in range(2)]
    third = [
        copy(10, buf.at[pl.ds(0, 2), 0, yl], to_y[0]),
        copy(11, buf.at[pl.ds(2, 2), 0, yr], to_y[1]),
        copy(12, buf.at[xl, 1, pl.ds(0, 2)], to_x[0]),
        copy(13, buf.at[xr, 1, pl.ds(2, 2)], to_x[1]),
    ]
    return first, second, third


def kernel(
    lengths, hidden, queries, key_w, value_w, out_w, result,
    xn, xb, kvw, part, part_in, win, qb, lo, wb, at, ob, acc, rb,
    kv_s, kv_r, wo_s, wo_r, sh_s, sh_r, x_s, x_r, q_s, q_r, p_s, p_r,
    win_s, win_r, at_s, at_r, ob_s, ob_r, loc,
):
    node, f = lax.axis_index("node"), lax.axis_index("fsdp")
    z, c = node // 2, lax.rem(node, 2)
    x, y = f // 4, lax.rem(f, 4)
    odd = lax.rem(z, 2)
    other = 1 - c
    half = odd
    pz = z + 1 - 2 * odd
    sz = lax.rem(z + 7 + 2 * odd, 8)
    band = lax.rem((z + 1) // 2, 2)
    sibling = (z * 2 + other, f)
    partner = (pz * 2 + c, f)
    cross = (pz * 2 + other, f)
    sharer = (sz * 2 + c, f)
    to_x = [(node, lax.rem(x + d, 4) * 4 + y) for d in (1, 3, 2)]
    to_y = [(node, x * 4 + lax.rem(y + d, 4)) for d in (1, 3, 2)]
    ahead = [(node, lax.rem(f + k, 16)) for k in range(1, 5)]
    behind = [(node, lax.rem(f + 16 - k, 16)) for k in range(1, 5)]
    place, peers = (x, y), (to_x, to_y)

    def remote(src, dst, ssem, rsem, device):
        return pltpu.make_async_remote_copy(
            src_ref=src, dst_ref=dst, send_sem=ssem, recv_sem=rsem, device_id=device, device_id_type=MESH
        )

    def start(copies):
        for copy in copies:
            copy.start()

    def arrive(copies):
        for copy in copies:
            copy.wait_recv()

    def sent(copies):
        for copy in copies:
            copy.wait_send()

    def chunk(s):
        if s == 0:
            return odd
        if s == SLOTS - 1:
            return 1 - odd
        return s + 1

    def band_col(s):
        return pl.multiple_of((band * 2 + c) * (SLOTS * COLS) + chunk(s) * COLS, COLS)

    local_kv = [
        pltpu.make_async_copy(
            w.at[pl.ds(half * 2, 2), :, pl.ds(pl.multiple_of(c * 256, 256), 256)],
            kvw.at[x, :, y, :, pl.ds(256 * i, 256)],
            loc.at[i],
        )
        for i, w in enumerate((key_w, value_w))
    ]
    start(local_kv)
    local_wo = [
        pltpu.make_async_copy(out_w.at[:, :, pl.ds(band_col(s), COLS)], wb.at[s, x, :, y], loc.at[2 + s])
        for s in range(SLOTS - 1)
    ]
    start(local_wo)
    local_q = pltpu.make_async_copy(
        queries.at[:, pl.ds(pl.multiple_of(c * 2048, 2048), 2048)], qb.at[c], loc.at[9]
    )
    local_q.start()

    barrier = pltpu.get_barrier_semaphore()
    greeted = [sibling, partner, cross, sharer] + to_x + to_y + ahead + behind
    for device in greeted:
        pl.semaphore_signal(barrier, inc=1, device_id=device, device_id_type=MESH)
    pl.semaphore_wait(barrier, len(greeted))

    kv1, kv2, kv3 = gather_copies(kvw, kv_s, kv_r, place, peers)
    wo = [gather_copies(wb.at[s], wo_s.at[s], wo_r.at[s], place, peers) for s in range(SLOTS - 1)]
    share = remote(wb.at[0], wb.at[SLOTS - 1], sh_s, sh_r, sharer)

    for copy in local_kv:
        copy.wait()
    start(kv1)
    send_q = remote(
        queries.at[:, pl.ds(pl.multiple_of(other * 2048, 2048), 2048)], qb.at[c], q_s.at[0], q_r.at[0], sibling
    )
    send_q.start()

    pos = f * TOK + lax.broadcasted_iota(jnp.int32, (TOK, 128), 0)
    end = jnp.int32(0)
    first = jnp.zeros((TOK, 128), jnp.int32)
    for e in range(8):
        end = end + lengths[0, e]
        first = jnp.where(pos >= end, end, first)
    lo[c] = (first - f * TOK + 4 * TOK).astype(F32)
    send_lo = remote(lo.at[c], lo.at[c], q_s.at[1], q_r.at[1], sibling)
    send_lo.start()

    @pl.loop(0, TOK // 16)
    def _(block):
        rows = pl.ds(pl.multiple_of(block * 16, 16), 16)
        h32 = hidden[rows, :].astype(F32)
        scale = lax.rsqrt(jnp.sum(h32 * h32, axis=1, keepdims=True) * (1.0 / 8192.0) + 1e-05)
        normed = (h32 * scale).astype(BF16)
        for fx in range(4):
            for fy in range(4):
                for hf in range(2):
                    for colour in range(2):
                        src = (fx * 4 + fy) * 512 + hf * 256 + colour * 128
                        dst = ((fx * 2 + colour) * 4 + fy) * 128
                        xn[hf, rows, pl.ds(dst, 128)] = normed[:, src:src + 128]

    send_x = [
        remote(xn.at[1 - half], xb.at[2 + c], x_s.at[0], x_r.at[0], partner),
        remote(xn.at[half], xb.at[c], x_s.at[1], x_r.at[1], sibling),
    ]
    start(send_x)
    local_x = pltpu.make_async_copy(xn.at[half], xb.at[c], loc.at[10])
    local_x.start()

    def wo_first(s):
        local_wo[s].wait()
        start(wo[s][0])

    def wo_second(s):
        arrive(wo[s][0])
        start(wo[s][1])

    def wo_third(s):
        arrive(wo[s][1])
        start(wo[s][2])

    def wo_done(s):
        arrive(wo[s][2])

    arrive(kv1)
    start(kv2)
    for s in range(3):
        wo_first(s)
    arrive(kv2)
    start(kv3)
    for s in range(3, SLOTS - 1):
        wo_first(s)
    send_x[0].wait_recv()
    pass_x = remote(xb.at[2 + c], xb.at[2 + c], x_s.at[2], x_r.at[2], sibling)
    pass_x.start()
    wo_second(0)
    arrive(kv3)
    wo_second(1)
    send_x[1].wait_recv()
    pass_x.wait_recv()
    local_x.wait()

    part[...] = jnp.zeros_like(part)

    @pl.loop(0, 4)
    def _(fx):
        w = kvw[fx].reshape(1024, 512)
        feats = pl.ds(pl.multiple_of(fx * 1024, 1024), 1024)
        for t in range(4):
            part[t] += jnp.dot(xb[t, :, feats], w, preferred_element_type=F32)

    send_p = remote(part.at[pl.ds(2, 2)], part_in, p_s.at[0], p_r.at[0], partner)
    send_p.start()
    wo_third(0)
    wo_second(2)
    send_p.wait_recv()
    for r in range(2):
        win[r, 4] = (part[r] + part_in[r]).astype(BF16)
    send_win = [
        remote(win.at[:, 4], win.at[:, 4 - k], win_s.at[k - 1], win_r.at[k - 1], ahead[k - 1]) for k in range(1, 5)
    ]
    start(send_win)
    wo_third(1)
    wo_second(3)
    local_q.wait()
    send_q.wait_recv()
    send_lo.wait_recv()
    arrive(send_win)

    col = lax.broadcasted_iota(jnp.int32, (TOK, 5 * TOK), 1)
    row = lax.broadcasted_iota(jnp.int32, (TOK, 5 * TOK), 0)

    def attend(j):
        @pl.loop(0, 8)
        def _(step):
            r, pair = step // 4, lax.rem(step, 4)
            both = qb[r, :, pl.ds(pl.multiple_of(j * 1024 + pair * 256, 256), 256)]
            q = jnp.concatenate([both[:, :HEAD], both[:, HEAD:]], axis=0)
            k = win[r, :, :, pl.ds(j * HEAD, HEAD)].reshape(5 * TOK, HEAD)
            v = win[r, :, :, pl.ds(256 + j * HEAD, HEAD)].reshape(5 * TOK, HEAD)
            allowed = ((col.astype(F32) >= lo[r][:, :1]) & (col <= row + 4 * TOK))[None]
            s = lax.dot_general(q, k, (((1,), (1,)), ((), ())), preferred_element_type=F32)
            s = (s * (HEAD ** -0.5)).reshape(2, TOK, 5 * TOK)
            s = jnp.where(allowed, s, F32(-1e30))
            top = jnp.max(s, axis=2, keepdims=True)
            w = jnp.where(allowed, jnp.exp(s - top), F32(0.0))
            total = jnp.sum(w, axis=2, keepdims=True)
            mixed = jnp.dot(w.astype(BF16).reshape(2 * TOK, 5 * TOK), v, preferred_element_type=F32)
            mixed = (mixed.reshape(2, TOK, HEAD) / total).astype(BF16)
            at[2 * c + j, r, :, pl.ds(pl.multiple_of(pair * HEAD, HEAD), HEAD)] = mixed[0]
            at[2 * c + j, r, :, pl.ds(pl.multiple_of((4 + pair) * HEAD, HEAD), HEAD)] = mixed[1]

        mine = at.at[2 * c + j, pl.ds(0, 2)]
        theirs = at.at[2 * c + j, pl.ds(2, 2)]
        copies = [
            remote(mine, theirs, at_s.at[3 * j], at_r.at[3 * j], partner),
            remote(mine, mine, at_s.at[3 * j + 1], at_r.at[3 * j + 1], sibling),
            remote(theirs, theirs, at_s.at[3 * j + 2], at_r.at[3 * j + 2], sibling),
        ]
        start(copies[:2])
        return copies

    def pass_on(copies):
        copies[0].wait_recv()
        copies[2].start()

    heads0 = attend(0)
    wo_third(2)
    wo_second(4)
    wo_done(0)
    share.start()
    heads1 = attend(1)
    wo_third(3)
    wo_second(5)
    pass_on(heads0)
    wo_third(4)
    wo_second(6)
    pass_on(heads1)
    for copies in (heads0, heads1):
        copies[1].wait_recv()
        copies[2].wait_recv()

    outs = []

    def project(s):
        acc[...] = jnp.zeros_like(acc)

        @pl.loop(0, 4)
        def _(g):
            acc[...] += jnp.dot(
                at[g].reshape(4 * TOK, 1024), wb[s, g].reshape(1024, COLS), preferred_element_type=F32
            )

        ob[s] = acc[...].astype(BF16).reshape(4, TOK, COLS)
        cols = pl.ds(band_col(s), COLS)
        rb[:, cols] = ob[s, c]
        copies = [
            remote(ob.at[s, slot], rb.at[:, cols], ob_s.at[s, i], ob_r.at[s, i], device)
            for i, (slot, device) in enumerate(((2 + c, partner), (2 + other, cross), (other, sibling)))
        ]
        start(copies)
        outs.extend(copies)

    project(0)
    wo_done(1)
    project(1)
    wo_third(5)
    wo_done(2)
    project(2)
    wo_done(3)
    project(3)
    wo_third(6)
    wo_done(4)
    project(4)
    wo_done(5)
    project(5)
    share.wait_recv()
    project(7)
    wo_done(6)
    project(6)
    arrive(outs)
    write = pltpu.make_async_copy(rb, result, loc.at[11])
    write.start()

    sent(kv1 + kv2 + kv3 + send_x + [pass_x, send_q, send_lo, send_p, share] + send_win + heads0 + heads1 + outs)
    for s in range(SLOTS - 1):
        for copies in wo[s]:
            sent(copies)
    write.wait()


def body(hidden, queries, key_matrix, value_matrix, out_weight, lengths):
    dma = pltpu.SemaphoreType.DMA
    vmem, anywhere = pl.BlockSpec(memory_space=pltpu.VMEM), pl.BlockSpec(memory_space=pl.ANY)
    projected = pl.pallas_call(
        kernel,
        out_shape=jax.ShapeDtypeStruct((TOK, 8192), BF16),
        in_specs=[pl.BlockSpec(memory_space=pltpu.SMEM), vmem] + [anywhere] * 4,
        out_specs=anywhere,
        scratch_shapes=[
            pltpu.VMEM((2, TOK, 4096), BF16),
            pltpu.VMEM((4, TOK, 4096), BF16),
            pltpu.VMEM((4, 2, 4, 128, 512), BF16),
            pltpu.VMEM((4, TOK, 512), F32),
            pltpu.VMEM((2, TOK, 512), F32),
            pltpu.VMEM((2, 5, TOK, 512), BF16),
            pltpu.VMEM((2, TOK, 2048), BF16),
            pltpu.VMEM((2, TOK, 128), F32),
            pltpu.VMEM((SLOTS, 4, 2, 4, 128, COLS), BF16),
            pltpu.VMEM((4, 4, TOK, 1024), BF16),
            pltpu.VMEM((SLOTS, 4, TOK, COLS), BF16),
            pltpu.VMEM((4 * TOK, COLS), F32),
            pltpu.VMEM((TOK, 8192), BF16),
            dma((14,)), dma((14,)),
            dma((SLOTS - 1, 14)), dma((SLOTS - 1, 14)),
            dma, dma,
            dma((3,)), dma((3,)),
            dma((2,)), dma((2,)),
            dma((1,)), dma((1,)),
            dma((4,)), dma((4,)),
            dma((6,)), dma((6,)),
            dma((SLOTS, 3)), dma((SLOTS, 3)),
            dma((12,)),
        ],
        compiler_params=pltpu.CompilerParams(
            collective_id=0, has_side_effects=True, vmem_limit_bytes=60 * 2 ** 20
        ),
        cost_estimate=pl.CostEstimate(flops=12 * 10 ** 9, bytes_accessed=16 * 2 ** 20, transcendentals=3 * 10 ** 6),
    )(
        lengths, hidden, queries,
        key_matrix.reshape(4, 128, 512), value_matrix.reshape(4, 128, 512), out_weight.reshape(2, 128, 8192),
    )
    return hidden.astype(F32) + projected.astype(F32)


def solution(mesh):
    placed = (
        P(("node", "fsdp"), None),
        P(("node", "fsdp"), None),
        P("fsdp", None),
        P("fsdp", None),
        P("fsdp", None),
        P("node", None),
    )
    return jax.shard_map(
        body, mesh=mesh, in_specs=placed, out_specs=P(("node", "fsdp"), None), check_vma=False
    )
```

time: 414 us -> 167 us (0.40)
  the two profiles are of different devices: /device:TPU:1 before, /device:TPU:29 now
where the time goes in v1:
time: 167 us
  Pallas kernels  163 us (98%)
  other arithmetic  4.12 us (2%)
    pallas_call x1, Pallas kernels, body(): pl.pallas_call(kernel, out_shape=jax.ShapeDtypeStruct((TOK, 8192), BF16),...  163 us
    add x1, other arithmetic, body(): return hidden.astype(F32) + projected.astype(F32)  4.12 us

profile of v1, /device:TPU:29, one launch (start us, length us, event | category | flops | bytes accessed | tf_op | source)
XLA Modules:
  0.0 166.8 jit_solution(4838276698958547997)
XLA Ops:
  0.0 0.0 copy-start
  0.0 162.7 %shard_map.64 = bf16[128,8192]{1,0:T(8,128)(2,1)} custom-call(s32[1,8]{1,0:T(1,128)} %lengths.1, bf16[128,8192]{1,0:T(8,128)(2,1)} %hidden.1, bf16[128,4096]{1,0:T(8,128)(2,1)} %queries.1, bf16[4,128,512]{2,1,0:T(8,128)(2,1)} %bitcast.4, bf16[4,128,512]{2,1,0:T(8,128)(2,1)} %bitcast.5, bf16[2,128,8192]{2,1,0:T(8,128)(2,1)} %bitcast.3), custom_call_target="tpu_custom_call" | custom-call | flops 12000000000 | bytes 16777216 | tf_op jit(solution)/shard_map/pallas_call | solution.py:328
  162.7 0.0 copy-done
  162.7 4.1 %convert_add_fusion = f32[128,8192]{1,0:T(8,128)} fusion(bf16[128,8192]{1,0:T(8,128)(2,1)} %shard_map.64, bf16[128,8192]{1,0:T(8,128)(2,1)S(1)} %copy-done), kind=kLoop, calls=%fused_computation | loop fusion | flops 3145728 | bytes 8388608 | tf_op jit(solution)/shard_map/add | solution.py:366
Async XLA Ops:
  0.0 162.7 %copy-start = (bf16[128,8192]{1,0:T(8,128)(2,1)S(1)}, bf16[128,8192]{1,0:T(8,128)(2,1)}, u32[]{:S(2)}) copy-start(bf16[128,8192]{1,0:T(8,128)(2,1)} %hidden.1) | copy-start | bytes 6291460

commit v2 on v1

v2 whole, which is shorter than its diff:
```python
import jax
import jax.numpy as jnp
from jax import lax
from jax.experimental import pallas as pl
from jax.experimental.pallas import tpu as pltpu
from jax.sharding import PartitionSpec as P

MESH = pl.DeviceIdType.MESH
HEAD = 128
TOK = 128
SLOTS = 8
COLS = 256
F32 = jnp.float32
BF16 = jnp.bfloat16


def gather_copies(piece, ssem, rsem, place, peers):
    x, y = place
    to_x, to_y = peers

    def copy(index, ref, device):
        return pltpu.make_async_remote_copy(
            src_ref=ref, dst_ref=ref, send_sem=ssem.at[index], recv_sem=rsem.at[index],
            device_id=device, device_id_type=MESH,
        )

    xr, xl = lax.rem(x + 1, 4), lax.rem(x + 3, 4)
    yr, yl = lax.rem(y + 1, 4), lax.rem(y + 3, 4)
    every, low, high = slice(None), pl.ds(0, 2), pl.ds(2, 2)
    first = [copy(k, piece(x, 0, y), to_x[k]) for k in range(3)]
    first += [copy(3 + k, piece(x, 1, y), to_y[k]) for k in range(3)]
    second = [copy(6 + k, piece(every, 0, y), to_y[k]) for k in range(2)]
    second += [copy(8 + k, piece(x, 1, every), to_x[k]) for k in range(2)]
    third = [
        copy(10, piece(low, 0, yl), to_y[0]),
        copy(11, piece(high, 0, yr), to_y[1]),
        copy(12, piece(xl, 1, low), to_x[0]),
        copy(13, piece(xr, 1, high), to_x[1]),
    ]
    return first, second, third


def kernel(
    lengths, hidden, queries, key_w, value_w, out_w, result,
    xn, xo, xz, kvw, part, part_z, part_in, win, qb, lo, wb, at, ob, acc, rb,
    kv_s, kv_r, wo_s, wo_r, sh_s, sh_r, x_s, x_r, q_s, q_r, p_s, p_r,
    win_s, win_r, at_s, at_r, ob_s, ob_r, loc,
):
    node, f = lax.axis_index("node"), lax.axis_index("fsdp")
    z, c = node // 2, lax.rem(node, 2)
    x, y = f // 4, lax.rem(f, 4)
    odd = lax.rem(z, 2)
    other = 1 - c
    pz = z + 1 - 2 * odd
    sz = lax.rem(z + 7 + 2 * odd, 8)
    band = lax.rem((z + 1) // 2, 2)
    sibling = (z * 2 + other, f)
    partner = (pz * 2 + c, f)
    cross = (pz * 2 + other, f)
    sharer = (sz * 2 + c, f)
    to_x = [(node, lax.rem(x + d, 4) * 4 + y) for d in (1, 3, 2)]
    to_y = [(node, x * 4 + lax.rem(y + d, 4)) for d in (1, 3, 2)]
    place, peers = (x, y), (to_x, to_y)

    def remote(src, dst, ssem, rsem, device):
        return pltpu.make_async_remote_copy(
            src_ref=src, dst_ref=dst, send_sem=ssem, recv_sem=rsem, device_id=device, device_id_type=MESH
        )

    flying, landed = [], set()

    def start(copies):
        for copy in copies:
            copy.start()
            flying.append(copy)

    def arrive(copies):
        for copy in copies:
            copy.wait_recv()
            landed.add(id(copy))

    def finish():
        for copy in flying:
            if id(copy) not in landed:
                copy.wait_recv()
        for copy in flying:
            copy.wait_send()

    def chunk(s):
        if s == 0:
            return odd
        if s == SLOTS - 1:
            return 1 - odd
        return s + 1

    def band_col(s):
        return pl.multiple_of((band * 2 + c) * (SLOTS * COLS) + chunk(s) * COLS, COLS)

    local_kv = [
        pltpu.make_async_copy(
            w.at[:, odd, :, pl.ds(pl.multiple_of(c * 256, 256), 256)],
            kvw.at[:, x, y, :, pl.ds(256 * i, 256)],
            loc.at[i],
        )
        for i, w in enumerate((key_w, value_w))
    ]
    for copy in local_kv:
        copy.start()
    local_wo = [
        pltpu.make_async_copy(out_w.at[:, :, pl.ds(band_col(s), COLS)], wb.at[s, x, :, y], loc.at[2 + s])
        for s in range(SLOTS - 1)
    ]
    for copy in local_wo:
        copy.start()
    local_q = pltpu.make_async_copy(
        queries.at[:, pl.ds(pl.multiple_of(c * 2048, 2048), 2048)], qb.at[c], loc.at[9]
    )
    local_q.start()

    barrier = pltpu.get_barrier_semaphore()
    greeted = [sibling, partner, cross, sharer] + to_x + to_y
    for device in greeted:
        pl.semaphore_signal(barrier, inc=1, device_id=device, device_id_type=MESH)
    pl.semaphore_wait(barrier, len(greeted))

    kv1, kv2, kv3 = gather_copies(lambda i, colour, k: kvw.at[colour, i, k], kv_s, kv_r, place, peers)
    wo = [
        gather_copies(lambda i, colour, k, s=s: wb.at[s, i, colour, k], wo_s.at[s], wo_r.at[s], place, peers)
        for s in range(SLOTS - 1)
    ]
    share = remote(wb.at[0], wb.at[SLOTS - 1], sh_s, sh_r, sharer)

    for copy in local_kv:
        copy.wait()
    start(kv1)
    send_q = remote(
        queries.at[:, pl.ds(pl.multiple_of(other * 2048, 2048), 2048)], qb.at[c], q_s.at[0], q_r.at[0], sibling
    )
    start([send_q])

    pos = f * TOK + lax.broadcasted_iota(jnp.int32, (TOK, 128), 0)
    end = jnp.int32(0)
    first = jnp.zeros((TOK, 128), jnp.int32)
    for e in range(8):
        end = end + lengths[0, e]
        first = jnp.where(pos >= end, end, first)
    lo[c] = (first - f * TOK + 4 * TOK).astype(F32)
    send_lo = remote(lo.at[c], lo.at[c], q_s.at[1], q_r.at[1], sibling)
    start([send_lo])

    @pl.loop(0, TOK // 16)
    def _(block):
        rows = pl.ds(pl.multiple_of(block * 16, 16), 16)
        h32 = hidden[rows, :].astype(F32)
        scale = lax.rsqrt(jnp.sum(h32 * h32, axis=1, keepdims=True) * (1.0 / 8192.0) + 1e-05)
        normed = (h32 * scale).astype(BF16)
        for owner in range(16):
            for quarter in range(4):
                src = owner * 512 + quarter * 128
                xn[quarter, rows, pl.ds(owner * 128, 128)] = normed[:, src:src + 128]

    send_x = [
        remote(xn.at[1 - odd], xz.at[0, c], x_s.at[0], x_r.at[0], partner),
        remote(xn.at[3 - odd], xz.at[1, c], x_s.at[1], x_r.at[1], sharer),
        remote(xn.at[odd], xo.at[0, c], x_s.at[2], x_r.at[2], sibling),
        remote(xn.at[2 + odd], xo.at[1, c], x_s.at[3], x_r.at[3], sibling),
    ]
    start(send_x)
    local_x = [pltpu.make_async_copy(xn.at[2 * i + odd], xo.at[i, c], loc.at[10 + i]) for i in range(2)]
    for copy in local_x:
        copy.start()

    def wo_first(s):
        local_wo[s].wait()
        start(wo[s][0])

    def wo_second_y(s):
        arrive(wo[s][0][:3])
        start(wo[s][1][:2])

    def wo_second_x(s):
        arrive(wo[s][0][3:])
        start(wo[s][1][2:])

    def wo_second(s):
        wo_second_x(s)
        wo_second_y(s)

    def wo_third(s):
        arrive(wo[s][1])
        start(wo[s][2])

    def wo_done(s):
        arrive(wo[s][2])

    arrive(kv1)
    start(kv2)
    wo_first(0)
    arrive(send_x[:2])
    pass_x = [remote(xz.at[i, c], xz.at[i, c], x_s.at[4 + i], x_r.at[4 + i], sibling) for i in range(2)]
    start(pass_x)
    arrive(kv2)
    start(kv3)
    wo_first(1)
    wo_first(2)
    arrive(send_x[2:])
    arrive(pass_x)
    for copy in local_x:
        copy.wait()
    arrive(kv3)

    def dot_kv(tokens, colour):
        return jnp.dot(
            tokens.reshape(2 * TOK, 2048), kvw[colour].reshape(2048, 512), preferred_element_type=F32
        ).reshape(2, TOK, 512)

    send_p = []
    for i, device in enumerate((partner, sharer)):
        part_z[i] = dot_kv(xz[i], i)
        send_p.append(remote(part_z.at[i], part_in.at[i], p_s.at[i], p_r.at[i], device))
        start(send_p[i:])
    part[...] = dot_kv(xo[0], 0)
    part[...] += dot_kv(xo[1], 1)

    wo_second(0)
    wo_first(3)
    wo_first(4)
    wo_third(0)
    arrive(send_p)
    total_kv = part[...] + part_in[0] + part_in[1]
    for j in range(2):
        for i in range(2):
            cols = slice(256 * i + HEAD * j, 256 * i + HEAD * (j + 1))
            win[j, :, 4, :, HEAD * i:HEAD * (i + 1)] = total_kv[:, :, cols].astype(BF16)
    send_win, pass_win, hops = [], [], (1, 3, 2)
    for j in range(2):
        send_win.append(remote(win.at[j, :, 4], win.at[j, :, 0], win_s.at[j, 0], win_r.at[j, 0], to_x[0]))
        pass_win.append([
            remote(
                win.at[j, :, jnp.where(y + d < 4, 4, 0)], win.at[j, :, 4 - d], win_s.at[j, d], win_r.at[j, d], to_y[k]
            )
            for k, d in enumerate(hops)
        ])

    def window_out(j):
        start(send_win[j:j + 1])
        for d, copy in zip(hops, pass_win[j]):
            pl.when(y + d < 4)(copy.start)
            flying.append(copy)

    def window_on(j):
        arrive(send_win[j:j + 1])
        for d, copy in zip(hops, pass_win[j]):
            pl.when(y + d >= 4)(copy.start)

    window_out(0)
    window_out(1)
    wo_second_x(1)
    wo_second_x(2)
    window_on(0)
    window_on(1)
    wo_second_y(1)
    wo_second_y(2)
    wo_done(0)
    start([share])
    wo_first(5)
    wo_first(6)
    local_q.wait()
    arrive([send_q])
    arrive([send_lo])
    arrive(pass_win[0])

    col = lax.broadcasted_iota(jnp.int32, (TOK, 5 * TOK), 1)
    row = lax.broadcasted_iota(jnp.int32, (TOK, 5 * TOK), 0)

    def attend(j):
        @pl.loop(0, 8)
        def _(step):
            r, pair = step // 4, lax.rem(step, 4)
            both = qb[r, :, pl.ds(pl.multiple_of(j * 1024 + pair * 256, 256), 256)]
            q = jnp.concatenate([both[:, :HEAD], both[:, HEAD:]], axis=0)
            k = win[j, r, :, :, pl.ds(0, HEAD)].reshape(5 * TOK, HEAD)
            v = win[j, r, :, :, pl.ds(HEAD, HEAD)].reshape(5 * TOK, HEAD)
            allowed = ((col.astype(F32) >= lo[r][:, :1]) & (col <= row + 4 * TOK))[None]
            s = lax.dot_general(q, k, (((1,), (1,)), ((), ())), preferred_element_type=F32)
            s = (s * (HEAD ** -0.5)).reshape(2, TOK, 5 * TOK)
            s = jnp.where(allowed, s, F32(-1e30))
            top = jnp.max(s, axis=2, keepdims=True)
            w = jnp.where(allowed, jnp.exp(s - top), F32(0.0))
            total = jnp.sum(w, axis=2, keepdims=True)
            mixed = jnp.dot(w.astype(BF16).reshape(2 * TOK, 5 * TOK), v, preferred_element_type=F32)
            mixed = (mixed.reshape(2, TOK, HEAD) / total).astype(BF16)
            at[2 * c + j, r, :, pl.ds(pl.multiple_of(pair * HEAD, HEAD), HEAD)] = mixed[0]
            at[2 * c + j, r, :, pl.ds(pl.multiple_of((4 + pair) * HEAD, HEAD), HEAD)] = mixed[1]

        mine = at.at[2 * c + j, pl.ds(0, 2)]
        theirs = at.at[2 * c + j, pl.ds(2, 2)]
        copies = [
            remote(mine, theirs, at_s.at[3 * j], at_r.at[3 * j], partner),
            remote(mine, mine, at_s.at[3 * j + 1], at_r.at[3 * j + 1], sibling),
            remote(theirs, theirs, at_s.at[3 * j + 2], at_r.at[3 * j + 2], sibling),
        ]
        start(copies[:2])
        return copies

    def pass_on(copies):
        arrive(copies[:1])
        start(copies[2:])

    heads0 = attend(0)
    wo_third(1)
    wo_second(3)
    arrive(pass_win[1])
    heads1 = attend(1)
    wo_third(2)
    wo_second(4)
    pass_on(heads0)
    wo_third(3)
    wo_second(5)
    pass_on(heads1)
    wo_third(4)
    wo_second(6)
    for copies in (heads0, heads1):
        arrive(copies[1:])

    outs = []

    def project(s):
        acc[...] = jnp.zeros_like(acc)

        @pl.loop(0, 4)
        def _(g):
            acc[...] += jnp.dot(
                at[g].reshape(4 * TOK, 1024), wb[s, g].reshape(1024, COLS), preferred_element_type=F32
            )

        ob[s] = acc[...].astype(BF16).reshape(4, TOK, COLS)
        cols = pl.ds(band_col(s), COLS)
        rb[:, cols] = ob[s, c]
        copies = [
            remote(ob.at[s, slot], rb.at[:, cols], ob_s.at[s, i], ob_r.at[s, i], device)
            for i, (slot, device) in enumerate(((2 + c, partner), (2 + other, cross), (other, sibling)))
        ]
        start(copies)
        outs.extend(copies)

    project(0)
    wo_done(1)
    project(1)
    wo_third(5)
    wo_done(2)
    project(2)
    wo_done(3)
    project(3)
    wo_third(6)
    wo_done(4)
    project(4)
    wo_done(5)
    project(5)
    arrive([share])
    project(7)
    wo_done(6)
    project(6)
    arrive(outs)
    write = pltpu.make_async_copy(rb, result, loc.at[12])
    write.start()

    finish()
    write.wait()


def body(hidden, queries, key_matrix, value_matrix, out_weight, lengths):
    dma = pltpu.SemaphoreType.DMA
    vmem, anywhere = pl.BlockSpec(memory_space=pltpu.VMEM), pl.BlockSpec(memory_space=pl.ANY)
    projected = pl.pallas_call(
        kernel,
        out_shape=jax.ShapeDtypeStruct((TOK, 8192), BF16),
        in_specs=[pl.BlockSpec(memory_space=pltpu.SMEM), vmem] + [anywhere] * 4,
        out_specs=anywhere,
        scratch_shapes=[
            pltpu.VMEM((4, TOK, 2048), BF16),
            pltpu.VMEM((2, 2, TOK, 2048), BF16),
            pltpu.VMEM((2, 2, TOK, 2048), BF16),
            pltpu.VMEM((2, 4, 4, 128, 512), BF16),
            pltpu.VMEM((2, TOK, 512), F32),
            pltpu.VMEM((2, 2, TOK, 512), F32),
            pltpu.VMEM((2, 2, TOK, 512), F32),
            pltpu.VMEM((2, 2, 5, TOK, 256), BF16),
            pltpu.VMEM((2, TOK, 2048), BF16),
            pltpu.VMEM((2, TOK, 128), F32),
            pltpu.VMEM((SLOTS, 4, 2, 4, 128, COLS), BF16),
            pltpu.VMEM((4, 4, TOK, 1024), BF16),
            pltpu.VMEM((SLOTS, 4, TOK, COLS), BF16),
            pltpu.VMEM((4 * TOK, COLS), F32),
            pltpu.VMEM((TOK, 8192), BF16),
            dma((14,)), dma((14,)),
            dma((SLOTS - 1, 14)), dma((SLOTS - 1, 14)),
            dma, dma,
            dma((6,)), dma((6,)),
            dma((2,)), dma((2,)),
            dma((2,)), dma((2,)),
            dma((2, 4)), dma((2, 4)),
            dma((6,)), dma((6,)),
            dma((SLOTS, 3)), dma((SLOTS, 3)),
            dma((13,)),
        ],
        compiler_params=pltpu.CompilerParams(
            collective_id=0, has_side_effects=True, vmem_limit_bytes=60 * 2 ** 20
        ),
        cost_estimate=pl.CostEstimate(flops=12 * 10 ** 9, bytes_accessed=16 * 2 ** 20, transcendentals=3 * 10 ** 6),
    )(
        lengths, hidden, queries,
        key_matrix.reshape(2, 2, 128, 512), value_matrix.reshape(2, 2, 128, 512), out_weight.reshape(2, 128, 8192),
    )
    return hidden.astype(F32) + projected.astype(F32)


def solution(mesh):
    placed = (
        P(("node", "fsdp"), None),
        P(("node", "fsdp"), None),
        P("fsdp", None),
        P("fsdp", None),
        P("fsdp", None),
        P("node", None),
    )
    return jax.shard_map(
        body, mesh=mesh, in_specs=placed, out_specs=P(("node", "fsdp"), None), check_vma=False
    )
```

time: 167 us -> 145 us (0.87)
  the two profiles are of different devices: /device:TPU:29 before, /device:TPU:1 now
where the time goes in v2:
time: 145 us; the launch traced here: 144 us
  Pallas kernels  140 us (97%)
  other arithmetic  4.12 us (3%)
    pallas_call x1, Pallas kernels, body(): pl.pallas_call(kernel, out_shape=jax.ShapeDtypeStruct((TOK, 8192), BF16),...  140 us
    add x1, other arithmetic, body(): return hidden.astype(F32) + projected.astype(F32)  4.12 us

profile of v2, /device:TPU:1, one launch (start us, length us, event | category | flops | bytes accessed | tf_op | source)
XLA Modules:
  0.0 144.3 jit_solution(6660905984443381347)
XLA Ops:
  0.0 0.0 copy-start
  0.0 140.2 %shard_map.64 = bf16[128,8192]{1,0:T(8,128)(2,1)} custom-call(s32[1,8]{1,0:T(1,128)} %lengths.1, bf16[128,8192]{1,0:T(8,128)(2,1)} %hidden.1, bf16[128,4096]{1,0:T(8,128)(2,1)} %queries.1, bf16[2,2,128,512]{3,2,1,0:T(8,128)(2,1)} %bitcast.4, bf16[2,2,128,512]{3,2,1,0:T(8,128)(2,1)} %bitcast.5, bf16[2,128,8192]{2,1,0:T(8,128)(2,1)} %bitcast.3), custom_call_target="tpu_custom_call" | custom-call | flops 12000000000 | bytes 16777216 | tf_op jit(solution)/shard_map/pallas_call | solution.py:375
  140.2 0.0 copy-done
  140.2 4.1 %convert_add_fusion = f32[128,8192]{1,0:T(8,128)} fusion(bf16[128,8192]{1,0:T(8,128)(2,1)} %shard_map.64, bf16[128,8192]{1,0:T(8,128)(2,1)S(1)} %copy-done), kind=kLoop, calls=%fused_computation | loop fusion | flops 3145728 | bytes 8388608 | tf_op jit(solution)/shard_map/add | solution.py:415
Async XLA Ops:
  0.0 140.2 %copy-start = (bf16[128,8192]{1,0:T(8,128)(2,1)S(1)}, bf16[128,8192]{1,0:T(8,128)(2,1)}, u32[]{:S(2)}) copy-start(bf16[128,8192]{1,0:T(8,128)(2,1)} %hidden.1) | copy-start | bytes 6291460

commit v3 on v2

--- a/solution.py
+++ b/solution.py
@@ -8,7 +8,7 @@
 MESH = pl.DeviceIdType.MESH
 HEAD = 128
 TOK = 128
-SLOTS = 8
+SLOTS = 6
 COLS = 256
 F32 = jnp.float32
 BF16 = jnp.bfloat16
@@ -43,7 +43,7 @@
 def kernel(
     lengths, hidden, queries, key_w, value_w, out_w, result,
     xn, xo, xz, kvw, part, part_z, part_in, win, qb, lo, wb, at, ob, acc, rb,
-    kv_s, kv_r, wo_s, wo_r, sh_s, sh_r, x_s, x_r, q_s, q_r, p_s, p_r,
+    kv_s, kv_r, wo_s, wo_r, x_s, x_r, q_s, q_r, p_s, p_r,
     win_s, win_r, at_s, at_r, ob_s, ob_r, loc,
 ):
     node, f = lax.axis_index("node"), lax.axis_index("fsdp")
@@ -53,11 +53,12 @@
     other = 1 - c
     pz = z + 1 - 2 * odd
     sz = lax.rem(z + 7 + 2 * odd, 8)
-    band = lax.rem((z + 1) // 2, 2)
+    uz, dz = lax.rem(z + 1, 8), lax.rem(z + 7, 8)
     sibling = (z * 2 + other, f)
     partner = (pz * 2 + c, f)
-    cross = (pz * 2 + other, f)
     sharer = (sz * 2 + c, f)
+    up, up_cross = (uz * 2 + c, f), (uz * 2 + other, f)
+    down, down_cross = (dz * 2 + c, f), (dz * 2 + other, f)
     to_x = [(node, lax.rem(x + d, 4) * 4 + y) for d in (1, 3, 2)]
     to_y = [(node, x * 4 + lax.rem(y + d, 4)) for d in (1, 3, 2)]
     place, peers = (x, y), (to_x, to_y)
@@ -86,15 +87,9 @@
         for copy in flying:
             copy.wait_send()
 
-    def chunk(s):
-        if s == 0:
-            return odd
-        if s == SLOTS - 1:
-            return 1 - odd
-        return s + 1
-
-    def band_col(s):
-        return pl.multiple_of((band * 2 + c) * (SLOTS * COLS) + chunk(s) * COLS, COLS)
+    def slot_col(s):
+        group = lax.rem(z + 24 - 3 * (s // 2), 8)
+        return pl.multiple_of(group * 1024 + c * 512 + (s % 2) * COLS, COLS)
 
     local_kv = [
         pltpu.make_async_copy(
@@ -107,18 +102,18 @@
     for copy in local_kv:
         copy.start()
     local_wo = [
-        pltpu.make_async_copy(out_w.at[:, :, pl.ds(band_col(s), COLS)], wb.at[s, x, :, y], loc.at[2 + s])
-        for s in range(SLOTS - 1)
+        pltpu.make_async_copy(out_w.at[:, :, pl.ds(slot_col(s), COLS)], wb.at[s, x, :, y], loc.at[2 + s])
+        for s in range(SLOTS)
     ]
     for copy in local_wo:
         copy.start()
     local_q = pltpu.make_async_copy(
-        queries.at[:, pl.ds(pl.multiple_of(c * 2048, 2048), 2048)], qb.at[c], loc.at[9]
+        queries.at[:, pl.ds(pl.multiple_of(c * 2048, 2048), 2048)], qb.at[c], loc.at[8]
     )
     local_q.start()
 
     barrier = pltpu.get_barrier_semaphore()
-    greeted = [sibling, partner, cross, sharer] + to_x + to_y
+    greeted = [sibling, up, up_cross, down, down_cross] + to_x + to_y
     for device in greeted:
         pl.semaphore_signal(barrier, inc=1, device_id=device, device_id_type=MESH)
     pl.semaphore_wait(barrier, len(greeted))
@@ -126,9 +121,8 @@
     kv1, kv2, kv3 = gather_copies(lambda i, colour, k: kvw.at[colour, i, k], kv_s, kv_r, place, peers)
     wo = [
         gather_copies(lambda i, colour, k, s=s: wb.at[s, i, colour, k], wo_s.at[s], wo_r.at[s], place, peers)
-        for s in range(SLOTS - 1)
+        for s in range(SLOTS)
     ]
-    share = remote(wb.at[0], wb.at[SLOTS - 1], sh_s, sh_r, sharer)
 
     for copy in local_kv:
         copy.wait()
@@ -261,10 +255,7 @@
     window_on(1)
     wo_second_y(1)
     wo_second_y(2)
-    wo_done(0)
-    start([share])
     wo_first(5)
-    wo_first(6)
     local_q.wait()
     arrive([send_q])
     arrive([send_lo])
@@ -290,22 +281,24 @@
             total = jnp.sum(w, axis=2, keepdims=True)
             mixed = jnp.dot(w.astype(BF16).reshape(2 * TOK, 5 * TOK), v, preferred_element_type=F32)
             mixed = (mixed.reshape(2, TOK, HEAD) / total).astype(BF16)
-            at[2 * c + j, r, :, pl.ds(pl.multiple_of(pair * HEAD, HEAD), HEAD)] = mixed[0]
-            at[2 * c + j, r, :, pl.ds(pl.multiple_of((4 + pair) * HEAD, HEAD), HEAD)] = mixed[1]
-
-        mine = at.at[2 * c + j, pl.ds(0, 2)]
-        theirs = at.at[2 * c + j, pl.ds(2, 2)]
+            at[2 * c + j, 2 + r, :, pl.ds(pl.multiple_of(pair * HEAD, HEAD), HEAD)] = mixed[0]
+            at[2 * c + j, 2 + r, :, pl.ds(pl.multiple_of((4 + pair) * HEAD, HEAD), HEAD)] = mixed[1]
+
+        above, mine, below = (at.at[2 * c + j, pl.ds(2 * i, 2)] for i in range(3))
         copies = [
-            remote(mine, theirs, at_s.at[3 * j], at_r.at[3 * j], partner),
-            remote(mine, mine, at_s.at[3 * j + 1], at_r.at[3 * j + 1], sibling),
-            remote(theirs, theirs, at_s.at[3 * j + 2], at_r.at[3 * j + 2], sibling),
+            remote(mine, below, at_s.at[j, 0], at_r.at[j, 0], up),
+            remote(mine, above, at_s.at[j, 1], at_r.at[j, 1], down),
+            remote(mine, mine, at_s.at[j, 2], at_r.at[j, 2], sibling),
+            remote(below, below, at_s.at[j, 3], at_r.at[j, 3], sibling),
+            remote(above, above, at_s.at[j, 4], at_r.at[j, 4], sibling),
         ]
-        start(copies[:2])
+        start(copies[:3])
         return copies
 
     def pass_on(copies):
-        arrive(copies[:1])
-        start(copies[2:])
+        for i in range(2):
+            arrive(copies[i:i + 1])
+            start(copies[3 + i:4 + i])
 
     heads0 = attend(0)
     wo_third(1)
@@ -318,49 +311,48 @@
     wo_third(3)
     wo_second(5)
     pass_on(heads1)
-    wo_third(4)
-    wo_second(6)
     for copies in (heads0, heads1):
-        arrive(copies[1:])
+        arrive(copies[2:])
 
     outs = []
 
     def project(s):
-        acc[...] = jnp.zeros_like(acc)
+        low = 0 if s < 4 else 2
+        rows = (6 - low) * TOK
+        acc[:rows] = jnp.zeros((rows, COLS), F32)
 
         @pl.loop(0, 4)
         def _(g):
-            acc[...] += jnp.dot(
-                at[g].reshape(4 * TOK, 1024), wb[s, g].reshape(1024, COLS), preferred_element_type=F32
+            acc[:rows] += jnp.dot(
+                at[g, low:].reshape(rows, 1024), wb[s, g].reshape(1024, COLS), preferred_element_type=F32
             )
 
-        ob[s] = acc[...].astype(BF16).reshape(4, TOK, COLS)
-        cols = pl.ds(band_col(s), COLS)
-        rb[:, cols] = ob[s, c]
+        ob[s, low:] = acc[:rows].astype(BF16).reshape(6 - low, TOK, COLS)
+        cols = pl.ds(slot_col(s), COLS)
+        rb[:, cols] = ob[s, 2 + c]
+        targets = [(4 + c, down), (4 + other, down_cross), (c, up), (other, up_cross), (2 + other, sibling)]
         copies = [
             remote(ob.at[s, slot], rb.at[:, cols], ob_s.at[s, i], ob_r.at[s, i], device)
-            for i, (slot, device) in enumerate(((2 + c, partner), (2 + other, cross), (other, sibling)))
+            for i, (slot, device) in enumerate(targets)
+            if low == 0 or i not in (2, 3)
         ]
         start(copies)
         outs.extend(copies)
 
+    wo_done(0)
     project(0)
+    wo_third(4)
     wo_done(1)
     project(1)
-    wo_third(5)
     wo_done(2)
     project(2)
+    wo_third(5)
     wo_done(3)
     project(3)
-    wo_third(6)
     wo_done(4)
     project(4)
     wo_done(5)
     project(5)
-    arrive([share])
-    project(7)
-    wo_done(6)
-    project(6)
     arrive(outs)
     write = pltpu.make_async_copy(rb, result, loc.at[12])
     write.start()
@@ -389,19 +381,18 @@
             pltpu.VMEM((2, TOK, 2048), BF16),
             pltpu.VMEM((2, TOK, 128), F32),
             pltpu.VMEM((SLOTS, 4, 2, 4, 128, COLS), BF16),
-            pltpu.VMEM((4, 4, TOK, 1024), BF16),
-            pltpu.VMEM((SLOTS, 4, TOK, COLS), BF16),
-            pltpu.VMEM((4 * TOK, COLS), F32),
+            pltpu.VMEM((4, 6, TOK, 1024), BF16),
+            pltpu.VMEM((SLOTS, 6, TOK, COLS), BF16),
+            pltpu.VMEM((6 * TOK, COLS), F32),
             pltpu.VMEM((TOK, 8192), BF16),
             dma((14,)), dma((14,)),
-            dma((SLOTS - 1, 14)), dma((SLOTS - 1, 14)),
-            dma, dma,
+            dma((SLOTS, 14)), dma((SLOTS, 14)),
             dma((6,)), dma((6,)),
             dma((2,)), dma((2,)),
             dma((2,)), dma((2,)),
             dma((2, 4)), dma((2, 4)),
-            dma((6,)), dma((6,)),
-            dma((SLOTS, 3)), dma((SLOTS, 3)),
+            dma((2, 5)), dma((2, 5)),
+            dma((SLOTS, 5)), dma((SLOTS, 5)),
             dma((13,)),
         ],
         compiler_params=pltpu.CompilerParams(

time: 145 us -> 133 us (0.917)
  Pallas kernels: 140 us -> 129 us
    pallas_call x1, Pallas kernels: 140 us -> 129 us  [body(): pl.pallas_call(kernel, out_shape=jax.ShapeDtypeStruct((TOK, 8192), BF16),...]
where the time goes in v3:
time: 133 us
  Pallas kernels  129 us (97%)
  other arithmetic  4.12 us (3%)
    pallas_call x1, Pallas kernels, body(): pl.pallas_call(kernel, out_shape=jax.ShapeDtypeStruct((TOK, 8192), BF16),...  129 us
    add x1, other arithmetic, body(): return hidden.astype(F32) + projected.astype(F32)  4.12 us

profile of v3, /device:TPU:1, one launch (start us, length us, event | category | flops | bytes accessed | tf_op | source)
XLA Modules:
  0.0 133.2 jit_solution(6604122369076057815)
XLA Ops:
  0.0 0.0 copy-start
  0.0 129.0 %shard_map.64 = bf16[128,8192]{1,0:T(8,128)(2,1)} custom-call(s32[1,8]{1,0:T(1,128)} %lengths.1, bf16[128,8192]{1,0:T(8,128)(2,1)} %hidden.1, bf16[128,4096]{1,0:T(8,128)(2,1)} %queries.1, bf16[2,2,128,512]{3,2,1,0:T(8,128)(2,1)} %bitcast.4, bf16[2,2,128,512]{3,2,1,0:T(8,128)(2,1)} %bitcast.5, bf16[2,128,8192]{2,1,0:T(8,128)(2,1)} %bitcast.3), custom_call_target="tpu_custom_call" | custom-call | flops 12000000000 | bytes 16777216 | tf_op jit(solution)/shard_map/pallas_call | solution.py:367
  129.0 0.0 copy-done
  129.0 4.1 %convert_add_fusion = f32[128,8192]{1,0:T(8,128)} fusion(bf16[128,8192]{1,0:T(8,128)(2,1)} %shard_map.64, bf16[128,8192]{1,0:T(8,128)(2,1)S(1)} %copy-done), kind=kLoop, calls=%fused_computation | loop fusion | flops 3145728 | bytes 8388608 | tf_op jit(solution)/shard_map/add | solution.py:406
Async XLA Ops:
  0.0 129.0 %copy-start = (bf16[128,8192]{1,0:T(8,128)(2,1)S(1)}, bf16[128,8192]{1,0:T(8,128)(2,1)}, u32[]{:S(2)}) copy-start(bf16[128,8192]{1,0:T(8,128)(2,1)} %hidden.1) | copy-start | bytes 6291460

commit v4 on v3

--- a/solution.py
+++ b/solution.py
@@ -37,7 +37,13 @@
         copy(12, piece(xl, 1, low), to_x[0]),
         copy(13, piece(xr, 1, high), to_x[1]),
     ]
-    return first, second, third
+    relay = [
+        copy(2, piece(xl, 0, y).at[pl.ds(0, 64)], to_x[0]),
+        copy(14, piece(xr, 0, y).at[pl.ds(64, 64)], to_x[1]),
+        copy(5, piece(x, 1, yl).at[pl.ds(0, 64)], to_y[0]),
+        copy(15, piece(x, 1, yr).at[pl.ds(64, 64)], to_y[1]),
+    ]
+    return first, second, third, relay
 
 
 def kernel(
@@ -93,22 +99,23 @@
 
     local_kv = [
         pltpu.make_async_copy(
-            w.at[:, odd, :, pl.ds(pl.multiple_of(c * 256, 256), 256)],
-            kvw.at[:, x, y, :, pl.ds(256 * i, 256)],
-            loc.at[i],
+            w.at[:, odd, :, pl.ds(pl.multiple_of((2 * c + j) * HEAD, HEAD), HEAD)],
+            kvw.at[:, x, y, :, pl.ds((2 * j + i) * HEAD, HEAD)],
+            loc.at[11 + 2 * j + i],
         )
         for i, w in enumerate((key_w, value_w))
+        for j in range(2)
     ]
     for copy in local_kv:
         copy.start()
     local_wo = [
-        pltpu.make_async_copy(out_w.at[:, :, pl.ds(slot_col(s), COLS)], wb.at[s, x, :, y], loc.at[2 + s])
+        pltpu.make_async_copy(out_w.at[:, :, pl.ds(slot_col(s), COLS)], wb.at[s, x, :, y], loc.at[s])
         for s in range(SLOTS)
     ]
     for copy in local_wo:
         copy.start()
     local_q = pltpu.make_async_copy(
-        queries.at[:, pl.ds(pl.multiple_of(c * 2048, 2048), 2048)], qb.at[c], loc.at[8]
+        queries.at[:, pl.ds(pl.multiple_of(c * 2048, 2048), 2048)], qb.at[c], loc.at[6]
     )
     local_q.start()
 
@@ -118,7 +125,7 @@
         pl.semaphore_signal(barrier, inc=1, device_id=device, device_id_type=MESH)
     pl.semaphore_wait(barrier, len(greeted))
 
-    kv1, kv2, kv3 = gather_copies(lambda i, colour, k: kvw.at[colour, i, k], kv_s, kv_r, place, peers)
+    kv1, kv2, kv3, _ = gather_copies(lambda i, colour, k: kvw.at[colour, i, k], kv_s, kv_r, place, peers)
     wo = [
         gather_copies(lambda i, colour, k, s=s: wb.at[s, i, colour, k], wo_s.at[s], wo_r.at[s], place, peers)
         for s in range(SLOTS)
@@ -160,20 +167,24 @@
         remote(xn.at[2 + odd], xo.at[1, c], x_s.at[3], x_r.at[3], sibling),
     ]
     start(send_x)
-    local_x = [pltpu.make_async_copy(xn.at[2 * i + odd], xo.at[i, c], loc.at[10 + i]) for i in range(2)]
+    local_x = [pltpu.make_async_copy(xn.at[2 * i + odd], xo.at[i, c], loc.at[7 + i]) for i in range(2)]
     for copy in local_x:
         copy.start()
 
     def wo_first(s):
         local_wo[s].wait()
-        start(wo[s][0])
+        start(wo[s][0][:2] + wo[s][0][3:5])
+
+    def wo_relay(s):
+        arrive(wo[s][0][:2] + wo[s][0][3:5])
+        start(wo[s][3])
 
     def wo_second_y(s):
-        arrive(wo[s][0][:3])
+        arrive(wo[s][3][:2])
         start(wo[s][1][:2])
 
     def wo_second_x(s):
-        arrive(wo[s][0][3:])
+        arrive(wo[s][3][2:])
         start(wo[s][1][2:])
 
     def wo_second(s):
@@ -195,6 +206,7 @@
     start(pass_x)
     arrive(kv2)
     start(kv3)
+    wo_relay(0)
     wo_first(1)
     wo_first(2)
     arrive(send_x[2:])
@@ -208,24 +220,21 @@
             tokens.reshape(2 * TOK, 2048), kvw[colour].reshape(2048, 512), preferred_element_type=F32
         ).reshape(2, TOK, 512)
 
-    send_p = []
+    send_p = [[], []]
     for i, device in enumerate((partner, sharer)):
-        part_z[i] = dot_kv(xz[i], i)
-        send_p.append(remote(part_z.at[i], part_in.at[i], p_s.at[i], p_r.at[i], device))
-        start(send_p[i:])
+        both = dot_kv(xz[i], i)
+        for j in range(2):
+            part_z[i, j] = both[:, :, 256 * j:256 * (j + 1)]
+            send_p[j].append(remote(part_z.at[i, j], part_in.at[i, j], p_s.at[i, j], p_r.at[i, j], device))
+            start(send_p[j][i:])
     part[...] = dot_kv(xo[0], 0)
     part[...] += dot_kv(xo[1], 1)
 
+    wo_relay(1)
     wo_second(0)
+    wo_relay(2)
     wo_first(3)
-    wo_first(4)
-    wo_third(0)
-    arrive(send_p)
-    total_kv = part[...] + part_in[0] + part_in[1]
-    for j in range(2):
-        for i in range(2):
-            cols = slice(256 * i + HEAD * j, 256 * i + HEAD * (j + 1))
-            win[j, :, 4, :, HEAD * i:HEAD * (i + 1)] = total_kv[:, :, cols].astype(BF16)
+
     send_win, pass_win, hops = [], [], (1, 3, 2)
     for j in range(2):
         send_win.append(remote(win.at[j, :, 4], win.at[j, :, 0], win_s.at[j, 0], win_r.at[j, 0], to_x[0]))
@@ -237,6 +246,9 @@
         ])
 
     def window_out(j):
+        arrive(send_p[j])
+        own = part[:, :, 256 * j:256 * (j + 1)] + part_in[0, j] + part_in[1, j]
+        win[j, :, 4] = own.astype(BF16)
         start(send_win[j:j + 1])
         for d, copy in zip(hops, pass_win[j]):
             pl.when(y + d < 4)(copy.start)
@@ -253,8 +265,12 @@
     wo_second_x(2)
     window_on(0)
     window_on(1)
+    wo_third(0)
+    wo_relay(3)
+    wo_first(4)
     wo_second_y(1)
     wo_second_y(2)
+    wo_relay(4)
     wo_first(5)
     local_q.wait()
     arrive([send_q])
@@ -301,49 +317,51 @@
             start(copies[3 + i:4 + i])
 
     heads0 = attend(0)
+    wo_relay(5)
+    wo_second(3)
+    wo_second(4)
     wo_third(1)
-    wo_second(3)
     arrive(pass_win[1])
     heads1 = attend(1)
+    wo_second(5)
+    pass_on(heads0)
     wo_third(2)
-    wo_second(4)
-    pass_on(heads0)
+    pass_on(heads1)
     wo_third(3)
-    wo_second(5)
-    pass_on(heads1)
     for copies in (heads0, heads1):
         arrive(copies[2:])
 
     outs = []
 
     def project(s):
-        low = 0 if s < 4 else 2
-        rows = (6 - low) * TOK
+        low, high = (2 if s >= 4 else 0), 6
+        rows = (high - low) * TOK
         acc[:rows] = jnp.zeros((rows, COLS), F32)
 
         @pl.loop(0, 4)
         def _(g):
             acc[:rows] += jnp.dot(
-                at[g, low:].reshape(rows, 1024), wb[s, g].reshape(1024, COLS), preferred_element_type=F32
+                at[g, low:high].reshape(rows, 1024), wb[s, g].reshape(1024, COLS), preferred_element_type=F32
             )
 
-        ob[s, low:] = acc[:rows].astype(BF16).reshape(6 - low, TOK, COLS)
+        ob[s, low:high] = acc[:rows].astype(BF16).reshape(high - low, TOK, COLS)
         cols = pl.ds(slot_col(s), COLS)
         rb[:, cols] = ob[s, 2 + c]
         targets = [(4 + c, down), (4 + other, down_cross), (c, up), (other, up_cross), (2 + other, sibling)]
+        slot_low = (4, 4, 0, 0, 2)
         copies = [
             remote(ob.at[s, slot], rb.at[:, cols], ob_s.at[s, i], ob_r.at[s, i], device)
             for i, (slot, device) in enumerate(targets)
-            if low == 0 or i not in (2, 3)
+            if low <= slot_low[i] < high
         ]
         start(copies)
         outs.extend(copies)
 
     wo_done(0)
     project(0)
-    wo_third(4)
     wo_done(1)
     project(1)
+    wo_third(4)
     wo_done(2)
     project(2)
     wo_third(5)
@@ -354,7 +372,7 @@
     wo_done(5)
     project(5)
     arrive(outs)
-    write = pltpu.make_async_copy(rb, result, loc.at[12])
+    write = pltpu.make_async_copy(rb, result, loc.at[9])
     write.start()
 
     finish()
@@ -375,8 +393,8 @@
             pltpu.VMEM((2, 2, TOK, 2048), BF16),
             pltpu.VMEM((2, 4, 4, 128, 512), BF16),
             pltpu.VMEM((2, TOK, 512), F32),
-            pltpu.VMEM((2, 2, TOK, 512), F32),
-            pltpu.VMEM((2, 2, TOK, 512), F32),
+            pltpu.VMEM((2, 2, 2, TOK, 256), F32),
+            pltpu.VMEM((2, 2, 2, TOK, 256), F32),
             pltpu.VMEM((2, 2, 5, TOK, 256), BF16),
             pltpu.VMEM((2, TOK, 2048), BF16),
             pltpu.VMEM((2, TOK, 128), F32),
@@ -385,15 +403,15 @@
             pltpu.VMEM((SLOTS, 6, TOK, COLS), BF16),
             pltpu.VMEM((6 * TOK, COLS), F32),
             pltpu.VMEM((TOK, 8192), BF16),
-            dma((14,)), dma((14,)),
-            dma((SLOTS, 14)), dma((SLOTS, 14)),
+            dma((16,)), dma((16,)),
+            dma((SLOTS, 16)), dma((SLOTS, 16)),
             dma((6,)), dma((6,)),
             dma((2,)), dma((2,)),
-            dma((2,)), dma((2,)),
+            dma((2, 2)), dma((2, 2)),
             dma((2, 4)), dma((2, 4)),
             dma((2, 5)), dma((2, 5)),
             dma((SLOTS, 5)), dma((SLOTS, 5)),
-            dma((13,)),
+            dma((15,)),
         ],
         compiler_params=pltpu.CompilerParams(
             collective_id=0, has_side_effects=True, vmem_limit_bytes=60 * 2 ** 20

time: 133 us -> 131 us (0.985)
  Pallas kernels: 129 us -> 127 us
    pallas_call x1, Pallas kernels: 129 us -> 127 us  [body(): pl.pallas_call(kernel, out_shape=jax.ShapeDtypeStruct((TOK, 8192), BF16),...]
where the time goes in v4:
time: 131 us
  Pallas kernels  127 us (97%)
  other arithmetic  4.12 us (3%)
    pallas_call x1, Pallas kernels, body(): pl.pallas_call(kernel, out_shape=jax.ShapeDtypeStruct((TOK, 8192), BF16),...  127 us
    add x1, other arithmetic, body(): return hidden.astype(F32) + projected.astype(F32)  4.12 us

profile of v4, /device:TPU:1, one launch (start us, length us, event | category | flops | bytes accessed | tf_op | source)
XLA Modules:
  0.0 130.8 jit_solution(2499797579027287596)
XLA Ops:
  0.0 0.0 copy-start
  0.0 126.7 %shard_map.64 = bf16[128,8192]{1,0:T(8,128)(2,1)} custom-call(s32[1,8]{1,0:T(1,128)} %lengths.1, bf16[128,8192]{1,0:T(8,128)(2,1)} %hidden.1, bf16[128,4096]{1,0:T(8,128)(2,1)} %queries.1, bf16[2,2,128,512]{3,2,1,0:T(8,128)(2,1)} %bitcast.4, bf16[2,2,128,512]{3,2,1,0:T(8,128)(2,1)} %bitcast.5, bf16[2,128,8192]{2,1,0:T(8,128)(2,1)} %bitcast.3), custom_call_target="tpu_custom_call" | custom-call | flops 12000000000 | bytes 16777216 | tf_op jit(solution)/shard_map/pallas_call | solution.py:385
  126.7 0.0 copy-done
  126.7 4.1 %convert_add_fusion = f32[128,8192]{1,0:T(8,128)} fusion(bf16[128,8192]{1,0:T(8,128)(2,1)} %shard_map.64, bf16[128,8192]{1,0:T(8,128)(2,1)S(1)} %copy-done), kind=kLoop, calls=%fused_computation | loop fusion | flops 3145728 | bytes 8388608 | tf_op jit(solution)/shard_map/add | solution.py:424
Async XLA Ops:
  0.0 126.7 %copy-start = (bf16[128,8192]{1,0:T(8,128)(2,1)S(1)}, bf16[128,8192]{1,0:T(8,128)(2,1)}, u32[]{:S(2)}) copy-start(bf16[128,8192]{1,0:T(8,128)(2,1)} %hidden.1) | copy-start | bytes 6291460

commit v5 on v4

--- a/solution.py
+++ b/solution.py
@@ -325,8 +325,8 @@
     heads1 = attend(1)
     wo_second(5)
     pass_on(heads0)
+    pass_on(heads1)
     wo_third(2)
-    pass_on(heads1)
     wo_third(3)
     for copies in (heads0, heads1):
         arrive(copies[2:])

time: 131 us -> 131 us (level)
  no operation moved by 1% of the time
where the time goes in v5:
time: 131 us
  Pallas kernels  127 us (97%)
  other arithmetic  4.12 us (3%)
    pallas_call x1, Pallas kernels, body(): pl.pallas_call(kernel, out_shape=jax.ShapeDtypeStruct((TOK, 8192), BF16),...  127 us
    add x1, other arithmetic, body(): return hidden.astype(F32) + projected.astype(F32)  4.12 us

profile of v5, /device:TPU:1, one launch (start us, length us, event | category | flops | bytes accessed | tf_op | source)
XLA Modules:
  0.0 130.8 jit_solution(4910505024307856034)
XLA Ops:
  0.0 0.0 copy-start
  0.0 126.6 %shard_map.64 = bf16[128,8192]{1,0:T(8,128)(2,1)} custom-call(s32[1,8]{1,0:T(1,128)} %lengths.1, bf16[128,8192]{1,0:T(8,128)(2,1)} %hidden.1, bf16[128,4096]{1,0:T(8,128)(2,1)} %queries.1, bf16[2,2,128,512]{3,2,1,0:T(8,128)(2,1)} %bitcast.4, bf16[2,2,128,512]{3,2,1,0:T(8,128)(2,1)} %bitcast.5, bf16[2,128,8192]{2,1,0:T(8,128)(2,1)} %bitcast.3), custom_call_target="tpu_custom_call" | custom-call | flops 12000000000 | bytes 16777216 | tf_op jit(solution)/shard_map/pallas_call | solution.py:385
  126.7 0.0 copy-done
  126.7 4.1 %convert_add_fusion = f32[128,8192]{1,0:T(8,128)} fusion(bf16[128,8192]{1,0:T(8,128)(2,1)} %shard_map.64, bf16[128,8192]{1,0:T(8,128)(2,1)S(1)} %copy-done), kind=kLoop, calls=%fused_computation | loop fusion | flops 3145728 | bytes 8388608 | tf_op jit(solution)/shard_map/add | solution.py:424
Async XLA Ops:
  0.0 126.7 %copy-start = (bf16[128,8192]{1,0:T(8,128)(2,1)S(1)}, bf16[128,8192]{1,0:T(8,128)(2,1)}, u32[]{:S(2)}) copy-start(bf16[128,8192]{1,0:T(8,128)(2,1)} %hidden.1) | copy-start | bytes 6291460
